TPU v7x, 256 devices: a whole 4x4x8 slice. The times are simulated.
256 devices in a mesh: rows: 32 (over y, z), own: 8 (over x, core).
Axes of the slice: x: 4, y: 4, z: 8, core: 2. Of those that a mesh axis runs over, the one named last changes fastest.
Arguments:
- embedding: bfloat16 [1048576, 128], P(('rows', 'own')), may hold values from -6 to 6
- assignment: int32 [1048576, 1], P(('rows', 'own')), may hold values from 0 to 1023; in each aligned block of 4096 rows (0 to 4095, 4096 to 8191, ...) at most 8 rows name the same one
- sub_logit: float32 [512], P('own'), may hold values from -1 to 1
- merge_offset: int32 [512], P(('own', 'rows')), may hold values from 1 to 7
Outputs:
- sub_prob: float32 [1048576], P(('rows', 'own'))
- split_score: float32 [512], P(('own', 'rows'))
- merge_score: float32 [512], P(('own', 'rows'))
Inputs may be any that keep to these rules, and one draw needn't show every extreme that they name: `assignment`: within the 4096 rows of one device (aligned blocks) no id is named by more than 8 rows, a bound that some block reaches; every id is named somewhere.
All inputs are finite; a program needn't handle non-finite values.
Results may differ from a plain program's by a relative error of at most 0.0003.
Values may be sent and summed in bfloat16 or wider, within the bound.
No kernel may reach another device: no remote copies, remote signals or barrier semaphores. Data moves between devices by JAX's collectives and lax.ppermute only.
A program may use at most 64 MiB of HBM per device.

v0:
```python
import math

import jax
import jax.numpy as jnp
from jax import lax
from jax.sharding import PartitionSpec as P

HIGH = lax.Precision.HIGHEST


def slot_table(expert, n_expert):
    total_rows = expert.shape[0]
    block_rows = min(256, total_rows)
    block_count = total_rows // block_rows
    expert_ids = jnp.arange(n_expert, dtype=jnp.int32)
    positions = jnp.arange(block_rows, dtype=jnp.int32)
    lower_tri = (positions[:, None] > positions[None, :]).astype(jnp.bfloat16)

    def step_block(running, block_e):
        hits = block_e[:, None] == expert_ids[None, :]
        onehot = hits.astype(jnp.bfloat16)
        earlier = jnp.dot(lower_tri, onehot, preferred_element_type=jnp.float32) + running[None, :]
        slot_rows = jnp.sum(jnp.where(hits, earlier, 0.0), axis=1)
        running = running + jnp.sum(onehot.astype(jnp.float32), axis=0)
        return (running, slot_rows.astype(jnp.int32))

    _, slot_blocks = lax.scan(
        step_block, jnp.zeros((n_expert,), jnp.float32), expert.reshape(block_count, block_rows)
    )
    return slot_blocks.reshape(-1)


def dispatch(rows_x, expert, n_expert, capacity):
    slot_index = slot_table(expert, n_expert)
    target = expert * capacity + slot_index
    buffer = jnp.zeros((n_expert * capacity, rows_x.shape[1]), rows_x.dtype).at[target].set(rows_x)
    filled = (
        jnp.zeros((n_expert * capacity,), jnp.bfloat16)
        .at[target]
        .set(jnp.ones(expert.shape, jnp.bfloat16))
    )
    return (buffer, filled, slot_index)


def read_back(table, expert, slot_index):
    n_expert, capacity = table.shape
    total_rows = expert.shape[0]
    block_rows = min(256, total_rows)
    block_count = total_rows // block_rows
    expert_ids = jnp.arange(n_expert, dtype=jnp.int32)
    slot_ids = jnp.arange(capacity, dtype=jnp.int32)

    def pick_block(carry, inputs):
        block_e, block_s = inputs
        onehot = (block_e[:, None] == expert_ids[None, :]).astype(jnp.float32)
        chosen = jnp.dot(onehot, table, precision=HIGH)
        values = jnp.sum(jnp.where(block_s[:, None] == slot_ids[None, :], chosen, 0.0), axis=1)
        return (carry, values)

    _, picked = lax.scan(
        pick_block,
        jnp.zeros((), jnp.int32),
        (expert.reshape(block_count, block_rows), slot_index.reshape(block_count, block_rows)),
    )
    return picked.reshape(-1)


def evidence_parts(second_mom, first_mom, counts):
    features = second_mom.shape[-1]
    identity_mat = jnp.eye(features, dtype=jnp.float32)
    kappa_post = 1.0 + counts
    scatter_psi = (
        identity_mat
        + second_mom
        - first_mom[..., :, None] * first_mom[..., None, :] / kappa_post[..., None, None]
    )
    factor = jnp.linalg.cholesky(scatter_psi)
    diagonal = jnp.diagonal(factor, axis1=-2, axis2=-1)
    logdet = 2.0 * jnp.sum(jnp.log(diagonal), axis=-1)
    prior_dof = features + 3.0
    half_steps = jnp.arange(features, dtype=jnp.float32) * 0.5
    gamma_part = jnp.sum(
        jax.scipy.special.gammaln((prior_dof + counts)[..., None] * 0.5 - half_steps)
        - jax.scipy.special.gammaln(prior_dof * 0.5 - half_steps),
        axis=-1,
    )
    evidence = (
        -0.5 * features * math.log(math.pi) * counts
        + gamma_part
        - 0.5 * (prior_dof + counts) * logdet
        - 0.5 * features * jnp.log(kappa_post)
    )
    return (factor, logdet, evidence)


def predictive(factor, logdet, counts, first_mom):
    features = factor.shape[-1]
    identity_mat = jnp.broadcast_to(jnp.eye(features, dtype=jnp.float32), factor.shape)
    inverse = jax.scipy.linalg.solve_triangular(factor, identity_mat, lower=True)
    whiten = jnp.sqrt(counts + 2.0)[..., None, None] * inverse
    center = first_mom / (1.0 + counts)[..., None]
    shifted = jnp.einsum("...fd,...d->...f", whiten, center, precision=HIGH)
    offset = 0.5 * features * jnp.log(counts + 2.0) - 0.5 * logdet
    return (whiten, shifted, offset)


def holder_stats(second_mom, first_mom, counts):
    features = second_mom.shape[-1]
    sub_factor, sub_logdet, sub_evid = evidence_parts(second_mom, first_mom, counts)
    whole_second = second_mom[:, 0] + second_mom[:, 1]
    whole_first = first_mom[:, 0] + first_mom[:, 1]
    whole_counts = counts[:, 0] + counts[:, 1]
    _, _, whole_evid = evidence_parts(whole_second, whole_first, whole_counts)
    whiten, shifted, offset = predictive(sub_factor, sub_logdet, counts, first_mom)
    gammaln = jax.scipy.special.gammaln
    split_score = (
        sub_evid[:, 0]
        + sub_evid[:, 1]
        - whole_evid
        + gammaln(counts[:, 0])
        + gammaln(counts[:, 1])
        - gammaln(whole_counts)
    ) / (features * features)
    return (
        whiten,
        shifted,
        offset,
        split_score,
        whole_second,
        whole_first,
        whole_counts,
        whole_evid,
    )


def merge_part(
    own_second, own_first, own_counts, own_evid, mate_second, mate_first, mate_counts, mate_evid
):
    features = own_second.shape[-1]
    _, _, merged_evid = evidence_parts(
        own_second + mate_second, own_first + mate_first, own_counts + mate_counts
    )
    gammaln = jax.scipy.special.gammaln
    return (
        merged_evid
        - own_evid
        - mate_evid
        + gammaln(own_counts + mate_counts)
        - gammaln(own_counts)
        - gammaln(mate_counts)
    ) / (features * features)


def score_slots(slots, whiten, shifted, offset, logits):
    sources = slots.shape[0]
    groups = min(8, sources)
    grouped = slots.reshape((groups, sources // groups) + slots.shape[1:])

    def one_group(group_rows):
        values = group_rows.astype(jnp.float32)
        image = jnp.einsum("iksad,ktfd->iksatf", values, whiten, precision=HIGH)
        image = image - shifted[None, :, None, None, :, :]
        energy = -0.5 * jnp.sum(image * image, axis=-1) + offset[None, :, None, None, :]
        return jax.nn.sigmoid(logits[None, :, None, None] + energy[..., 1] - energy[..., 0])

    return lax.map(one_group, grouped).reshape(slots.shape[:4])


def shards(embedding, assignment, sub_logit, merge_offset):
    features = embedding.shape[1]
    owners = lax.axis_size("own")
    local_k = sub_logit.shape[0]
    per_holder = merge_offset.shape[0]
    clusters = local_k * owners
    capacity = max(2, embedding.shape[0] // clusters)
    expert = assignment[:, 0]
    buffer, filled, slot_index = dispatch(embedding, expert, 2 * clusters, capacity)
    outgoing = buffer.reshape(owners, local_k, 2, capacity, features)
    outgoing_mask = filled.reshape(owners, local_k, 2, capacity)
    arrived, present = (
        lax.all_to_all(outgoing, "own", split_axis=0, concat_axis=0, tiled=True),
        lax.all_to_all(outgoing_mask, "own", split_axis=0, concat_axis=0, tiled=True),
    )
    second_mom = jnp.einsum(
        "iksad,iksaf->ksdf", arrived, arrived, preferred_element_type=jnp.float32
    )
    first_mom = jnp.einsum("iksa,iksad->ksd", present, arrived, preferred_element_type=jnp.float32)
    counts = jnp.sum(present.astype(jnp.float32), axis=(0, 3))
    second_mom, first_mom, counts = (
        lax.psum_scatter(second_mom, "rows", scatter_dimension=0, tiled=True),
        lax.psum_scatter(first_mom, "rows", scatter_dimension=0, tiled=True),
        lax.psum_scatter(counts, "rows", scatter_dimension=0, tiled=True),
    )
    holder_out = holder_stats(second_mom, first_mom, counts)
    whiten, shifted, offset = (
        lax.all_gather(holder_out[0], "rows", axis=0, tiled=True),
        lax.all_gather(holder_out[1], "rows", axis=0, tiled=True),
        lax.all_gather(holder_out[2], "rows", axis=0, tiled=True),
    )
    sub_odds = score_slots(arrived, whiten, shifted, offset, sub_logit)
    returned = lax.all_to_all(sub_odds, "own", split_axis=0, concat_axis=0, tiled=True)
    sub_prob = read_back(returned.reshape(2 * clusters, capacity), expert, slot_index)
    all_second, all_first, all_counts, all_evid = (
        lax.all_gather(holder_out[4], "own", axis=0, tiled=True),
        lax.all_gather(holder_out[5], "own", axis=0, tiled=True),
        lax.all_gather(holder_out[6], "own", axis=0, tiled=True),
        lax.all_gather(holder_out[7], "own", axis=0, tiled=True),
    )
    partner = (lax.axis_index("own") + merge_offset) % owners
    picker = (partner[:, None] == jnp.arange(owners, dtype=jnp.int32)[None, :]).astype(jnp.float32)
    mate_second = jnp.einsum(
        "jq,qjde->jde",
        picker,
        all_second.reshape(owners, per_holder, features, features),
        precision=HIGH,
    )
    mate_first = jnp.einsum(
        "jq,qjd->jd", picker, all_first.reshape(owners, per_holder, features), precision=HIGH
    )
    mate_counts = jnp.einsum(
        "jq,qj->j", picker, all_counts.reshape(owners, per_holder), precision=HIGH
    )
    mate_evid = jnp.einsum("jq,qj->j", picker, all_evid.reshape(owners, per_holder), precision=HIGH)
    merge_score = merge_part(
        holder_out[4],
        holder_out[5],
        holder_out[6],
        holder_out[7],
        mate_second,
        mate_first,
        mate_counts,
        mate_evid,
    )
    return (sub_prob, holder_out[3], merge_score)


def solution(mesh):
    in_specs = (P(("rows", "own"), None), P(("rows", "own"), None), P("own"), P(("own", "rows")))
    out_specs = (P(("rows", "own")), P(("own", "rows")), P(("own", "rows")))
    return jax.shard_map(shards, mesh=mesh, in_specs=in_specs, out_specs=out_specs, check_vma=False)
```

profile of v0, /device:TPU:1, one launch (start us, length us, event | category | flops | bytes accessed | tf_op | source)
XLA Modules:
  0.0 719.4 jit_solution(17111839819931471397)
XLA Ops:
  9.1 12.2 %while.36 = (s32[]{:T(128)}, f32[1024]{0:T(1024)S(1)}, s32[16,256]{1,0:T(8,128)S(1)}, s32[16,256]{1,0:T(8,128)S(1)}, s32[]{:T(128)}, /*index=5*/s32[]{:T(128)}) while((s32[]{:T(128)}, f32[1024]{0:T(1024)S(1)}, s32[16,256]{1,0:T(8,128)S(1)}, s32[16,256]{1,0:T(8,128)S(1)}, s32[]{:T(128)}, /*index=5*/s32[]{:T(128)}) %tuple.92), condition=%wide.region_3.4_spmd.clone, body=%wide.region_0.3_spmd.clone.sunk | while | flops 136709120 | bytes 33879 | solution.py:27
  21.4 28.6 %scatter_custom_fusion.1 = bf16[8192]{0:T(1024)(128)(2,1)S(1)} fusion(s32[4096]{0:T(1024)S(1)} %bitcast.310, bf16[4096]{0:T(1024)(128)(2,1)S(1)} %broadcast.878, bf16[]{:T(256)} %constant.138.clone.1), kind=kCustom, calls=%fused_computation.90 | custom fusion | bytes 16386 | tf_op jit(solution)/shard_map/scatter | solution.py:40
  51.2 6.5 all-to-all-start.1
  57.6 12.8 %scatter_custom_fusion = bf16[8192,128]{1,0:T(8,128)(2,1)} fusion(s32[4096]{0:T(1024)S(1)} %bitcast.311, bf16[4096,128]{1,0:T(8,128)(2,1)} %param.11, bf16[]{:T(256)} %constant.138.clone.1), kind=kCustom, calls=%fused_computation.53 | custom fusion | bytes 2097664 | tf_op jit(solution)/shard_map/scatter | solution.py:36
  70.4 4.8 all-to-all-start
  75.9 25.7 %all-to-all-done = bf16[8,64,2,8,128]{4,3,2,1,0:T(8,128)(2,1)S(1)} async-done(((bf16[8,64,2,8,128]{4,3,2,1,0:T(8,128)(2,1)}), bf16[8,64,2,8,128]{4,3,2,1,0:T(8,128)(2,1)S(1)}, u32[]{:S(2)}, u32[]{:S(2)}) %all-to-all-start) | async-done | bytes 2097184 | tf_op jit(solution)/shard_map/all_to_all | solution.py:181
  110.5 66.1 %all-reduce.2 = f32[64,2]{0,1:T(2,128)S(1)} all-reduce(f32[64,2]{0,1:T(2,128)S(1)} %convert_reduce_fusion.1), channel_id=5, replica_groups=mesh['rows'=32,'own'=8] {'rows'}, use_global_device_ids=true, to_apply=%region_7.8.clone | all-reduce | flops 128 | bytes 1024
  177.0 145.8 %all-reduce.8.cloned.1.call-done = (f32[64,2,128,128]{2,3,0,1:T(8,128)}, f32[64,2,128]{2,0,1:T(8,128)}) async-done(((f32[64,2,128,128]{2,3,0,1:T(8,128)}, f32[64,2,128]{2,0,1:T(8,128)}), (f32[64,2,128,128]{2,3,0,1:T(8,128)}, f32[64,2,128]{2,0,1:T(8,128)})) %all-reduce.8.cloned.1.call-update) | async-done | bytes 8454160
  329.2 46.9 %custom-call.11 = f32[2,2,128,128]{3,2,1,0:T(8,128)S(1)} custom-call(f32[2,2,128,128]{3,2,1,0:T(8,128)S(1)} %fusion.48), custom_call_target="Cholesky" | custom-call | tf_op jit(solution)/shard_map/jit(cholesky)/cholesky | solution.py:77
  376.4 11.4 %copy.179 = f32[2,2,128,128]{1,0,3,2:T(2,128)} copy(f32[2,2,128,128]{3,2,1,0:T(8,128)S(1)} %get-tuple-element.275) | data formatting | bytes 524288 | tf_op jit(solution)/shard_map/jit(cholesky)/select_n | solution.py:77
  387.9 39.3 %custom-call.12 = f32[2,2,1,128,128]{3,4,2,1,0:T(8,128)S(1)} custom-call(f32[2,2,1,128,128]{4,3,2,1,0:T(8,128)S(1)} %get-tuple-element.274), custom_call_target="InvertDiagBlocksLowerTriangular" | custom-call | tf_op jit(solution)/shard_map/jit(_solve_triangular)/vmap(vmap())/triangular_solve | solution.py:99
  427.2 6.7 gather_fusion
  437.0 12.6 %all-reduce = f32[16]{0:T(128)S(1)} all-reduce(f32[16]{0:T(128)S(1)} %bitcast_dynamic-update-slice_fusion), channel_id=2, replica_groups=mesh['rows'=32,'own'=8] {'own'}, use_global_device_ids=true, to_apply=%add | all-reduce | flops 16 | bytes 128
  450.1 23.5 %custom-call.21 = f32[2,128,128]{2,1,0:T(8,128)S(1)} custom-call(f32[2,128,128]{2,1,0:T(8,128)S(1)} %fusion.53), custom_call_target="Cholesky" | custom-call | tf_op jit(solution)/shard_map/jit(cholesky)/cholesky | solution.py:77
  473.6 35.9 %all-gather.3 = f32[32,2,2]{2,1,0:T(2,128)S(1)} all-gather(f32[1,2,2]{2,1,0:T(2,128)S(1)} %get-tuple-element.281), channel_id=1, replica_groups=mesh['rows'=32,'own'=8] {'rows'}, dimensions={0}, use_global_device_ids=true | all-gather | bytes 528 | tf_op jit(solution)/shard_map/all_gather | solution.py:198
  510.2 16.9 %all-gather.2 = f32[16,1,128]{2,1,0:T(1,128)S(1)} all-gather(f32[2,1,128]{2,1,0:T(1,128)S(1)} %bitcast.316), channel_id=4, replica_groups=mesh['rows'=32,'own'=8] {'own'}, dimensions={0}, use_global_device_ids=true | all-gather | bytes 9216 | tf_op jit(solution)/shard_map/all_gather | solution.py:205
  528.6 34.4 %all_gather.22 = f32[64,2,128]{2,1,0:T(2,128)S(1)} all-gather(f32[2,2,128]{2,1,0:T(2,128)S(1)} %bitcast.314), channel_id=1, replica_groups=mesh['rows'=32,'own'=8] {'rows'}, dimensions={0}, use_global_device_ids=true | all-gather | bytes 67584 | tf_op jit(solution)/shard_map/all_gather | solution.py:197
  566.7 23.5 %custom-call.22 = f32[2,128,128]{2,1,0:T(8,128)S(1)} custom-call(f32[2,128,128]{2,1,0:T(8,128)S(1)} %fusion.50), custom_call_target="Cholesky" | custom-call | tf_op jit(solution)/shard_map/jit(cholesky)/cholesky | solution.py:77
  590.5 4.7 copy.187
  597.1 24.6 %all-reduce.1 = f32[16]{0:T(128)S(1)} all-reduce(f32[16]{0:T(128)S(1)} %get-tuple-element.266), channel_id=1, replica_groups=mesh['rows'=32,'own'=8] {'own'}, use_global_device_ids=true, to_apply=%add.1 | all-reduce | flops 16 | bytes 128
  621.8 4.7 copy.191
  628.9 60.1 %while.34 = (s32[]{:T(128)}, f32[8,1,64,2,8]{2,4,3,1,0:T(8,128)S(1)}, f32[64]{0:T(128)S(1)}, bf16[8,1,64,2,8,128]{5,4,3,2,1,0:T(8,128)(2,1)S(1)}, f32[64,2,128,1...) while((s32[]{:T(128)}, f32[8,1,64,2,8]{2,4,3,1,0:T(8,128)S(1)}, ...), condition=%wide.region_15.16_spmd, body=%wide.region_13.15_spmd.sunk | while | flops 403446784 | bytes 8782941 | solution.py:166
  628.9 7.4 %fusion.130 = f32[64,2,2,8]{3,1,2,0:T(2,128)S(1)} fusion(f32[64,2,128,128]{3,2,1,0:T(8,128)} %get-tuple-element.439, f32[64,2,128]{2,1,0:T(2,128)S(1)} %get-tuple-element.440, bf16[8,1,64,2,8,128]{5,4,3,2,1,0:T(8,128)(2,1)S(1)} %get-tuple-element.438, s32[]{:T(128)} %get-tuple-element.427), kind=kOutput, calls=%fused_computation.14.clone.1 | convolution fusion | flops 403437568 | bytes 8724484 | tf_op jit(solution)/shard_map/while/body/eval_jaxpr/iksad,ktfd->iksatf/dot_general | solution.py:161
  636.4 7.4 %fusion.130 = f32[64,2,2,8]{3,1,2,0:T(2,128)S(1)} fusion(f32[64,2,128,128]{3,2,1,0:T(8,128)} %get-tuple-element.439, f32[64,2,128]{2,1,0:T(2,128)S(1)} %get-tuple-element.440, bf16[8,1,64,2,8,128]{5,4,3,2,1,0:T(8,128)(2,1)S(1)} %get-tuple-element.438, s32[]{:T(128)} %get-tuple-element.427), kind=kOutput, calls=%fused_computation.14.clone.1 | convolution fusion | flops 403437568 | bytes 8724484 | tf_op jit(solution)/shard_map/while/body/eval_jaxpr/iksad,ktfd->iksatf/dot_general | solution.py:161
  643.9 7.4 %fusion.130 = f32[64,2,2,8]{3,1,2,0:T(2,128)S(1)} fusion(f32[64,2,128,128]{3,2,1,0:T(8,128)} %get-tuple-element.439, f32[64,2,128]{2,1,0:T(2,128)S(1)} %get-tuple-element.440, bf16[8,1,64,2,8,128]{5,4,3,2,1,0:T(8,128)(2,1)S(1)} %get-tuple-element.438, s32[]{:T(128)} %get-tuple-element.427), kind=kOutput, calls=%fused_computation.14.clone.1 | convolution fusion | flops 403437568 | bytes 8724484 | tf_op jit(solution)/shard_map/while/body/eval_jaxpr/iksad,ktfd->iksatf/dot_general | solution.py:161
  651.4 7.4 %fusion.130 = f32[64,2,2,8]{3,1,2,0:T(2,128)S(1)} fusion(f32[64,2,128,128]{3,2,1,0:T(8,128)} %get-tuple-element.439, f32[64,2,128]{2,1,0:T(2,128)S(1)} %get-tuple-element.440, bf16[8,1,64,2,8,128]{5,4,3,2,1,0:T(8,128)(2,1)S(1)} %get-tuple-element.438, s32[]{:T(128)} %get-tuple-element.427), kind=kOutput, calls=%fused_computation.14.clone.1 | convolution fusion | flops 403437568 | bytes 8724484 | tf_op jit(solution)/shard_map/while/body/eval_jaxpr/iksad,ktfd->iksatf/dot_general | solution.py:161
  658.9 7.4 %fusion.130 = f32[64,2,2,8]{3,1,2,0:T(2,128)S(1)} fusion(f32[64,2,128,128]{3,2,1,0:T(8,128)} %get-tuple-element.439, f32[64,2,128]{2,1,0:T(2,128)S(1)} %get-tuple-element.440, bf16[8,1,64,2,8,128]{5,4,3,2,1,0:T(8,128)(2,1)S(1)} %get-tuple-element.438, s32[]{:T(128)} %get-tuple-element.427), kind=kOutput, calls=%fused_computation.14.clone.1 | convolution fusion | flops 403437568 | bytes 8724484 | tf_op jit(solution)/shard_map/while/body/eval_jaxpr/iksad,ktfd->iksatf/dot_general | solution.py:161
  666.4 7.4 %fusion.130 = f32[64,2,2,8]{3,1,2,0:T(2,128)S(1)} fusion(f32[64,2,128,128]{3,2,1,0:T(8,128)} %get-tuple-element.439, f32[64,2,128]{2,1,0:T(2,128)S(1)} %get-tuple-element.440, bf16[8,1,64,2,8,128]{5,4,3,2,1,0:T(8,128)(2,1)S(1)} %get-tuple-element.438, s32[]{:T(128)} %get-tuple-element.427), kind=kOutput, calls=%fused_computation.14.clone.1 | convolution fusion | flops 403437568 | bytes 8724484 | tf_op jit(solution)/shard_map/while/body/eval_jaxpr/iksad,ktfd->iksatf/dot_general | solution.py:161
  674.0 7.4 %fusion.130 = f32[64,2,2,8]{3,1,2,0:T(2,128)S(1)} fusion(f32[64,2,128,128]{3,2,1,0:T(8,128)} %get-tuple-element.439, f32[64,2,128]{2,1,0:T(2,128)S(1)} %get-tuple-element.440, bf16[8,1,64,2,8,128]{5,4,3,2,1,0:T(8,128)(2,1)S(1)} %get-tuple-element.438, s32[]{:T(128)} %get-tuple-element.427), kind=kOutput, calls=%fused_computation.14.clone.1 | convolution fusion | flops 403437568 | bytes 8724484 | tf_op jit(solution)/shard_map/while/body/eval_jaxpr/iksad,ktfd->iksatf/dot_general | solution.py:161
  681.5 7.4 %fusion.130 = f32[64,2,2,8]{3,1,2,0:T(2,128)S(1)} fusion(f32[64,2,128,128]{3,2,1,0:T(8,128)} %get-tuple-element.439, f32[64,2,128]{2,1,0:T(2,128)S(1)} %get-tuple-element.440, bf16[8,1,64,2,8,128]{5,4,3,2,1,0:T(8,128)(2,1)S(1)} %get-tuple-element.438, s32[]{:T(128)} %get-tuple-element.427), kind=kOutput, calls=%fused_computation.14.clone.1 | convolution fusion | flops 403437568 | bytes 8724484 | tf_op jit(solution)/shard_map/while/body/eval_jaxpr/iksad,ktfd->iksatf/dot_general | solution.py:161
  694.2 4.2 all-to-all-done.2
  700.2 11.8 %while.35 = (s32[]{:T(128)}, f32[16,256]{1,0:T(8,128)S(1)}, s32[16,256]{1,0:T(8,128)S(1)}, s32[16,256]{1,0:T(8,128)S(1)}, f32[1024,8]{0,1:T(8,128)S(1)}, /*index=5*/s32[]{:T(128)}, s32[]{:T(128)}) while((s32[]{:T(128)}, f32[16,256]{1,0:T(8,128)S(1)}, s32[16,256]{1,0:T(8,128)S(1)}, s32[16,256]{1,0:T(8,128)S(1)}, ...), condition=%wide.region_18.19_spmd.clone, body=%wide.region_16.18_spmd.clone.sunk | while | flops 25433856 | bytes 42069 | solution.py:60
  (282 shorter events, 63.6 us)
Async XLA Ops:
  7.2 14.2 %copy-start = (s32[4096,1]{0,1:T(1,128)S(1)}, s32[4096,1]{0,1:T(1,128)}, u32[]{:S(2)}) copy-start(s32[4096,1]{0,1:T(1,128)} %param.12) | copy-start | bytes 49156
  51.2 19.3 %all-to-all-start.1 = ((bf16[8,2,512]{2,1,0:T(2,128)(2,1)}), bf16[8,2,512]{2,1,0:T(2,128)(2,1)S(1)}, u32[]{:S(2)}, u32[]{:S(2)}) async-start(bf16[8,2,512]{2,1,0:T(2,128)(2,1)} %reshape.438), calls=%async_computation.1 | async-start | bytes 32768 | tf_op jit(solution)/shard_map/all_to_all | solution.py:182
  70.4 31.2 %all-to-all-start = ((bf16[8,64,2,8,128]{4,3,2,1,0:T(8,128)(2,1)}), bf16[8,64,2,8,128]{4,3,2,1,0:T(8,128)(2,1)S(1)}, u32[]{:S(2)}, u32[]{:S(2)}) async-start(bf16[8,64,2,8,128]{4,3,2,1,0:T(8,128)(2,1)} %bitcast.294), calls=%async_computation | async-start | bytes 4194304 | tf_op jit(solution)/shard_map/all_to_all | solution.py:181
  75.3 247.5 %all-reduce.8.cloned.1.call-start = ((), (), s32[]{:S(2)}) async-start(), calls=%async_computation.5 | async-start | bytes 16908288
  108.5 0.7 copy-start.4
  108.5 455.5 %all-gather.9.cloned.1.call-start = ((), (), s32[]{:S(2)}) async-start(), calls=%async_computation.4 | async-start | bytes 1179648 | tf_op jit(solution)/shard_map/all_gather | solution.py:204
  325.3 303.5 %all-gather.7.cloned.1.call-start = ((), (), s32[]{:S(2)}) async-start(), calls=%async_computation.3 | async-start | bytes 8650752 | tf_op jit(solution)/shard_map/all_gather | solution.py:196
  376.4 59.0 %copy-start.2 = (s32[2]{0:T(128)S(1)}, s32[2]{0:T(128)}, u32[]{:S(2)}) copy-start(s32[2]{0:T(128)} %param.14) | copy-start | bytes 28
  376.4 59.2 %copy-start.3 = (u32[256]{0:T(256)S(1)}, u32[256]{0:T(256)}, u32[]{:S(2)}) copy-start(u32[256]{0:T(256)} %constant.357) | copy-start | bytes 3076
  590.5 38.4 %copy-start.1 = (f32[64]{0:T(128)S(1)}, f32[64]{0:T(128)}, u32[]{:S(2)}) copy-start(f32[64]{0:T(128)} %param.13) | copy-start | bytes 772
  689.7 8.6 %all-to-all-start.2 = ((f32[8,1,1024]{2,1,0:T(1,128)}), f32[8,1,1024]{2,1,0:T(1,128)S(1)}, u32[]{:S(2)}, u32[]{:S(2)}) async-start(f32[8,1,1024]{2,1,0:T(1,128)} %reshape.440), calls=%async_computation.2 | async-start | bytes 65536 | tf_op jit(solution)/shard_map/all_to_all | solution.py:201
Sparse Core Ops, SparseCore 0:
  108.6 214.1 all-reduce.7
  325.5 25.1 all-gather.8
  435.5 97.3 all-gather.6
where the time goes:
time: 729 us; the launch traced here: 719 us
  blocking collectives  191 us (26%)
  waiting for transfers between devices  176 us (24%)
  other arithmetic  149 us (20%)
  local copies, waits for them, and re-layouts  87.4 us (12%)
  matrix products  84.1 us (12%)
  starting transfers between devices  15.7 us (2%)
  between operations  15.7 us (2%)
    unnamed x4, waiting for transfers between devices  146 us
    unnamed x3, blocking collectives  103 us
    another operation x9, other arithmetic, evidence_parts(): factor = jnp.linalg.cholesky(scatter_psi)  94.2 us
    dot_general x8, matrix products, one_group(): image = jnp.einsum('iksad,ktfd->iksatf', values, whiten, precision=HIGH)  59 us
    another operation x3, other arithmetic, predictive(): jax.scipy.linalg.solve_triangular(factor, identity_mat, lower=True)  39.4 us
    all_gather x1, blocking collectives, shards(): lax.all_gather(holder_out[2], 'rows', axis=0, tiled=True)  35.9 us
    all_gather x1, blocking collectives, shards(): lax.all_gather(holder_out[1], 'rows', axis=0, tiled=True)  34.4 us
    scatter x1, local copies, waits for them, and re-layouts, dispatch(): filled = jnp.zeros((n_expert * capacity,), jnp.bfloat16).at[target].set(j...  28.6 us
  transfers between devices with their start and end apart: 6, of which 3 were waited for; matrix products, arithmetic and copies ran while one was open for 27% of the time, Pallas kernels for 0%

commit v1 on v0

v1 whole, which is shorter than its diff:
```python
import math

import jax
import jax.numpy as jnp
from jax import lax
from jax.experimental import pallas as pl
from jax.experimental.pallas import tpu as pltpu
from jax.sharding import PartitionSpec as P

D = 128
CAP = 8
EMPTY = 64.0
VMEM_LIMIT = 48 * 1024 * 1024
PANEL = 16


def iota(shape, dim):
    return lax.broadcasted_iota(jnp.int32, shape, dim)


def split3(value):
    high = value.astype(jnp.bfloat16)
    rest = value - high.astype(jnp.float32)
    middle = rest.astype(jnp.bfloat16)
    low = (rest - middle.astype(jnp.float32)).astype(jnp.bfloat16)
    return high, middle, low


def slots_of(labels):
    blocks = labels.shape[0]
    flipped = jnp.transpose(labels.astype(jnp.float32))
    before = iota((128, 128), 0) < iota((128, 128), 1)
    lanes = iota((128, 128), 1)
    levels = iota((8, 128), 0)
    running = jnp.zeros((8, 128), jnp.float32)
    rows = []
    for b in range(blocks):
        across = labels[b : b + 1, :]
        down = jnp.broadcast_to(flipped[:, b : b + 1], (128, 128)).astype(jnp.int32)
        same = jnp.where((down == across) & before, 1.0, 0.0)
        inside = jnp.sum(same, axis=0, keepdims=True)
        low = across & 127
        upper = levels == (across >> 7)
        found = jnp.take_along_axis(running, jnp.broadcast_to(low, (8, 128)), axis=1)
        earlier = jnp.sum(jnp.where(upper, found, 0.0), axis=0, keepdims=True)
        rows.append(across * CAP + (inside + earlier).astype(jnp.int32))
        hot_low = jnp.where((down & 127) == lanes, 1.0, 0.0).astype(jnp.bfloat16)
        hot_up = jnp.where(upper, 1.0, 0.0).astype(jnp.bfloat16)
        running = running + jnp.dot(hot_up, hot_low, preferred_element_type=jnp.float32)
    return jnp.concatenate(rows, axis=0)


def dispatch_kernel(labels_ref, rows_ref, target_ref, out_ref, wide, table, places, sem):
    target_ref[...] = slots_of(labels_ref[...])
    copy = pltpu.make_async_copy(target_ref, places, sem)
    copy.start()
    wide[...] = rows_ref[...].astype(jnp.float32)
    table[...] = jnp.full(table.shape, EMPTY, jnp.float32)
    copy.wait()

    def block(b, carry):
        for j in range(128):
            table[pl.ds(places[b, j], 1), :] = wide[pl.ds(b * 128 + j, 1), :]
        return carry

    lax.fori_loop(0, labels_ref.shape[0], block, 0)
    out_ref[...] = table[...].astype(jnp.bfloat16)


def dispatch(embedding, labels, slots):
    total = embedding.shape[0]
    return pl.pallas_call(
        dispatch_kernel,
        out_shape=(
            jax.ShapeDtypeStruct(labels.shape, jnp.int32),
            jax.ShapeDtypeStruct((slots, D), jnp.bfloat16),
        ),
        in_specs=[pl.BlockSpec(memory_space=pltpu.VMEM)] * 2,
        out_specs=[pl.BlockSpec(memory_space=pltpu.VMEM)] * 2,
        scratch_shapes=[
            pltpu.VMEM((total, D), jnp.float32),
            pltpu.VMEM((slots, D), jnp.float32),
            pltpu.SMEM(labels.shape, jnp.int32),
            pltpu.SemaphoreType.DMA,
        ],
        compiler_params=pltpu.CompilerParams(vmem_limit_bytes=VMEM_LIMIT),
    )(labels, embedding)


def eliminate(work, count):
    pivots = [[] for _ in range(count)]
    lanes = iota((PANEL, D), 1)
    down = iota((PANEL, D), 0)
    for p in range(D // PANEL):
        base = p * PANEL
        tiles = [work[m, base : base + PANEL, :] for m in range(count)]
        diag = [jnp.ones((PANEL, D), jnp.float32) for _ in range(count)]
        for i in range(PANEL):
            j = base + i
            at_col = lanes == j
            for m in range(count):
                tile = tiles[m]
                column = jnp.broadcast_to(tile[:, j : j + 1], (PANEL, D))
                pivot = column[i : i + 1, :]
                factor = jnp.where(down > i, column * (1.0 / pivot), 0.0)
                diag[m] = jnp.where(down == i, pivot, diag[m])
                edge = jnp.where(down == i, 1.0, -factor)
                tiles[m] = jnp.where(at_col, edge, tile - factor * tile[i : i + 1, :])
        for m in range(count):
            pivots[m].append(diag[m])
            work[m, base : base + PANEL, :] = tiles[m]
            below = base + PANEL
            if below < D:
                e1, e2, e3 = split3(tiles[m])
                n1, n2, n3 = split3(tiles[m] * (1.0 / diag[m]))
                left = jnp.concatenate([n1, n1, n2, n2, n1, n3], axis=0)
                right = jnp.concatenate([e1, e2, e1, e2, e3, e1], axis=0)
                step = lax.dot_general(
                    left,
                    right,
                    (((0,), (0,)), ((), ())),
                    preferred_element_type=jnp.float32,
                )
                old = work[m, below:, :]
                wide_lanes = iota(old.shape, 1)
                inside = (wide_lanes >= base) & (wide_lanes < below)
                work[m, below:, :] = jnp.where(inside, 0.0, old) - step[below:, :]
    return pivots


def log_sum(pivot_tiles):
    total = jnp.zeros((1, D), jnp.float32)
    for tile in pivot_tiles:
        total = total + jnp.sum(jnp.log(tile), axis=0, keepdims=True)
    return total


def posterior_scatter(second, first, number):
    same = iota((D, D), 0) == iota((D, D), 1)
    over = jnp.broadcast_to(first, (D, D))
    return jnp.where(same, 1.0, 0.0) + second - jnp.transpose(over) * over / (1.0 + number)


def factor_kernel(logit_ref, rows_ref, xt_ref, maps_ref, shift_ref, const_ref, pack_ref, info_ref, work):
    sources = rows_ref.shape[0]
    depth = sources * 16
    moments = []
    for c in range(2):
        rows = rows_ref[:, 16 * c : 16 * c + 16, :].reshape(depth, D)
        empty = rows.astype(jnp.float32) > 8.0
        clean = jnp.where(empty, 0.0, rows.astype(jnp.float32)).astype(jnp.bfloat16)
        valid = jnp.where(empty, 0.0, 1.0).astype(jnp.bfloat16)
        turned = jnp.transpose(clean)
        xt_ref[c] = turned
        zero_side = (iota((D, depth), 1) & 8) == 0
        none = jnp.zeros_like(turned)
        left = jnp.concatenate(
            [jnp.where(zero_side, turned, none), jnp.where(zero_side, none, turned)], axis=0
        )
        second = jnp.dot(left, clean, preferred_element_type=jnp.float32)
        side = ((iota((16, depth), 1) >> 3) & 1) == (iota((16, depth), 0) & 1)
        pick = jnp.where(side, 1.0, 0.0).astype(jnp.bfloat16)
        first = jnp.dot(pick, clean, preferred_element_type=jnp.float32)
        number = jnp.dot(pick, valid, preferred_element_type=jnp.float32)
        for s in range(2):
            moments.append((second[s * D : (s + 1) * D], first[s : s + 1], number[s : s + 1]))
    for c in range(2):
        moments.append(tuple(a + b for a, b in zip(moments[2 * c], moments[2 * c + 1])))
    for m in range(6):
        work[m] = posterior_scatter(*moments[m])
    lower = iota((D, D), 0) >= iota((D, D), 1)
    same = iota((D, D), 0) == iota((D, D), 1)
    pack_ref[0:D, :] = jnp.where(lower, moments[4][0], moments[5][0])
    diagonal = jnp.sum(jnp.where(same, moments[5][0], 0.0), axis=0, keepdims=True)

    pivots = eliminate(work, 6)

    logdets = [log_sum(tiles) for tiles in pivots]
    tail = [diagonal, moments[4][1], moments[5][1], moments[4][2], moments[5][2]]
    pack_ref[D : D + 8, :] = jnp.concatenate(
        tail + [logdets[4], logdets[5], jnp.zeros((1, D), jnp.float32)], axis=0
    )
    info_ref[...] = jnp.concatenate(
        [moments[m][2] for m in range(4)] + logdets[:4], axis=0
    )
    for c in range(2):
        offsets = []
        for t in range(2):
            m = 2 * c + t
            _, first, number = moments[m]
            spread = jnp.concatenate(pivots[m], axis=0)
            unit = jnp.where(lower, work[m], 0.0)
            whiten = jnp.sqrt(number + 2.0) * (unit * lax.rsqrt(spread))
            center = first / (1.0 + number)
            shifted = jnp.sum(whiten * center, axis=1, keepdims=True)
            shift_ref[c, t * D : (t + 1) * D, :] = jnp.broadcast_to(shifted, (D, D))
            for k, piece in enumerate(split3(whiten)):
                maps_ref[c, k, t * D : (t + 1) * D, :] = piece
            offsets.append(0.5 * D * jnp.log(number + 2.0) - 0.5 * logdets[m])
        const_ref[c] = jnp.broadcast_to(logit_ref[c] + (offsets[1] - offsets[0]), (8, D))


def factor(logits, arrived):
    sources = arrived.shape[0]
    depth = sources * 16
    f32 = jnp.float32
    return pl.pallas_call(
        factor_kernel,
        out_shape=(
            jax.ShapeDtypeStruct((2, D, depth), jnp.bfloat16),
            jax.ShapeDtypeStruct((2, 3, 2 * D, D), jnp.bfloat16),
            jax.ShapeDtypeStruct((2, 2 * D, D), f32),
            jax.ShapeDtypeStruct((2, 8, D), f32),
            jax.ShapeDtypeStruct((D + 8, D), f32),
            jax.ShapeDtypeStruct((8, D), f32),
        ),
        in_specs=[
            pl.BlockSpec(memory_space=pltpu.SMEM),
            pl.BlockSpec(memory_space=pltpu.VMEM),
        ],
        out_specs=[pl.BlockSpec(memory_space=pltpu.VMEM)] * 6,
        scratch_shapes=[pltpu.VMEM((6, D, D), f32)],
        compiler_params=pltpu.CompilerParams(vmem_limit_bytes=VMEM_LIMIT),
    )(logits, arrived)


def score_kernel(xt_ref, maps_ref, shift_ref, const_ref, out_ref):
    columns = xt_ref[...]
    image = jnp.dot(maps_ref[2], columns, preferred_element_type=jnp.float32)
    image = image + jnp.dot(maps_ref[1], columns, preferred_element_type=jnp.float32)
    image = image + jnp.dot(maps_ref[0], columns, preferred_element_type=jnp.float32)
    image = image - shift_ref[:, 0:1]
    squares = image * image
    total0 = jnp.sum(squares[:D], axis=0, keepdims=True)
    total1 = jnp.sum(squares[D:], axis=0, keepdims=True)
    odds = const_ref[0:1, 0:1] + 0.5 * (total0 - total1)
    out_ref[...] = 1.0 / (1.0 + jnp.exp(-odds))


def score(xt, maps, shift, const):
    clusters, _, depth = xt.shape
    width = min(512, depth)
    return pl.pallas_call(
        score_kernel,
        out_shape=jax.ShapeDtypeStruct((clusters, 1, depth), jnp.float32),
        grid=(clusters, depth // width),
        in_specs=[
            pl.BlockSpec((None, D, width), lambda c, w: (c, 0, w)),
            pl.BlockSpec((None, 3, 2 * D, D), lambda c, w: (c, 0, 0, 0)),
            pl.BlockSpec((None, 2 * D, D), lambda c, w: (c, 0, 0)),
            pl.BlockSpec((None, 8, D), lambda c, w: (c, 0, 0)),
        ],
        out_specs=pl.BlockSpec((None, 1, width), lambda c, w: (c, 0, w)),
        compiler_params=pltpu.CompilerParams(vmem_limit_bytes=VMEM_LIMIT),
    )(xt, maps, shift, const)


def unpack(pack):
    body = pack[0:D]
    flipped = jnp.transpose(body)
    low = iota((D, D), 0) > iota((D, D), 1)
    same = iota((D, D), 0) == iota((D, D), 1)
    second0 = jnp.where(low, body, flipped)
    second1 = jnp.where(same, pack[D : D + 1], jnp.where(low, flipped, body))
    return (
        (second0, pack[D + 1 : D + 2], pack[D + 3 : D + 4], pack[D + 5 : D + 6]),
        (second1, pack[D + 2 : D + 3], pack[D + 4 : D + 5], pack[D + 6 : D + 7]),
    )


def merge_kernel(mate_ref, own_ref, mate0_ref, mate1_ref, out_ref, work):
    own = unpack(own_ref[...])
    mates = (unpack(mate0_ref[...])[0], unpack(mate1_ref[...])[1])
    for c in range(2):
        work[c] = posterior_scatter(*(own[c][k] + mates[c][k] for k in range(3)))
    pivots = eliminate(work, 2)
    out_ref[...] = jnp.concatenate(
        [mates[c][2] for c in range(2)]
        + [mates[c][3] for c in range(2)]
        + [log_sum(pivots[c]) for c in range(2)]
        + [jnp.zeros((2, D), jnp.float32)],
        axis=0,
    )


def merge(mate, own, everyone):
    block = (None,) + own.shape
    return pl.pallas_call(
        merge_kernel,
        out_shape=jax.ShapeDtypeStruct((8, D), jnp.float32),
        grid_spec=pltpu.PrefetchScalarGridSpec(
            num_scalar_prefetch=1,
            grid=(1,),
            in_specs=[
                pl.BlockSpec(own.shape, lambda g, mate: (0, 0)),
                pl.BlockSpec(block, lambda g, mate: (mate[0], 0, 0)),
                pl.BlockSpec(block, lambda g, mate: (mate[1], 0, 0)),
            ],
            out_specs=pl.BlockSpec((8, D), lambda g, mate: (0, 0)),
            scratch_shapes=[pltpu.VMEM((2, D, D), jnp.float32)],
        ),
        compiler_params=pltpu.CompilerParams(vmem_limit_bytes=VMEM_LIMIT),
    )(mate, own, everyone, everyone)


def read_kernel(table_ref, target_ref, out_ref):
    target = target_ref[...]
    upper = target >> 7
    low = target & 127
    for g in range(target.shape[0] // 8):
        part = slice(8 * g, 8 * g + 8)
        total = jnp.zeros((8, 128), jnp.float32)
        for k in range(table_ref.shape[0]):
            line = jnp.broadcast_to(table_ref[k : k + 1, :], (8, 128))
            found = jnp.take_along_axis(line, low[part], axis=1)
            total = jnp.where(upper[part] == k, found, total)
        out_ref[part, :] = total


def read_back(table, target):
    return pl.pallas_call(
        read_kernel,
        out_shape=jax.ShapeDtypeStruct(target.shape, jnp.float32),
    )(table, target)


def evidence(numbers, logdets):
    prior = D + 3.0
    half_steps = jnp.arange(D, dtype=jnp.float32) * 0.5
    gammaln = jax.scipy.special.gammaln
    gamma_part = jnp.sum(
        gammaln((prior + numbers)[:, None] * 0.5 - half_steps) - gammaln(prior * 0.5 - half_steps),
        axis=-1,
    )
    return (
        -0.5 * D * math.log(math.pi) * numbers
        + gamma_part
        - 0.5 * (prior + numbers) * logdets
        - 0.5 * D * jnp.log(1.0 + numbers)
    )


def scores(info, pack, merged):
    sub_n, sub_logdet = info[0:4, 0], info[4:8, 0]
    whole_n, whole_logdet = pack[D + 3 : D + 5, 0], pack[D + 5 : D + 7, 0]
    mate_n, mate_logdet, both_logdet = merged[0:2, 0], merged[2:4, 0], merged[4:6, 0]
    numbers = jnp.concatenate([sub_n, whole_n, mate_n, whole_n + mate_n])
    logdets = jnp.concatenate([sub_logdet, whole_logdet, mate_logdet, both_logdet])
    value = evidence(numbers, logdets)
    value = value + jax.scipy.special.gammaln(numbers)
    split = (value[0:4].reshape(2, 2).sum(axis=1) - value[4:6]) / (D * D)
    join = (value[8:10] - value[4:6] - value[6:8]) / (D * D)
    return split, join


def shards(embedding, assignment, sub_logit, merge_offset):
    owners, holders = lax.axis_size("own"), lax.axis_size("rows")
    experts = 2 * owners * sub_logit.shape[0]
    axes = ("own", "rows")
    devices = owners * holders
    labels = assignment.reshape(-1, 128)
    target, outgoing = dispatch(embedding, labels, experts * CAP)
    per_holder = merge_offset.shape[0]
    chunk = 2 * per_holder * CAP
    arrived = lax.all_to_all(
        outgoing.reshape(devices, chunk, D), axes, split_axis=0, concat_axis=0, tiled=True
    )
    logits = lax.dynamic_slice(sub_logit, (lax.axis_index("rows") * per_holder,), (per_holder,))
    xt, maps, shift, const, pack, info = factor(logits, arrived)
    everyone = lax.all_gather(pack, "own", axis=0, tiled=False)
    odds = score(xt, maps, shift, const)
    outward = odds.reshape(per_holder, devices, 2 * CAP).transpose(1, 0, 2).reshape(devices, chunk)
    returned = lax.all_to_all(outward, axes, split_axis=0, concat_axis=0, tiled=True)
    mate = (lax.axis_index("own") + merge_offset) % owners
    merged = merge(mate, pack, everyone)
    split, join = scores(info, pack, merged)
    sub_prob = read_back(returned.reshape(-1, 128), target).reshape(-1)
    return (sub_prob, split, join)


def solution(mesh):
    in_specs = (P(("rows", "own"), None), P(("rows", "own"), None), P("own"), P(("own", "rows")))
    out_specs = (P(("rows", "own")), P(("own", "rows")), P(("own", "rows")))
    return jax.shard_map(shards, mesh=mesh, in_specs=in_specs, out_specs=out_specs, check_vma=False)
```

time: 729 us -> 157 us (0.22); the launches traced: 719 us -> 157 us
  blocking collectives: 191 us -> 13.1 us
  other arithmetic: 149 us -> 2.55 us
  waiting for transfers between devices: 176 us -> 66.6 us
  matrix products: 84.1 us -> 0 us
  local copies, waits for them, and re-layouts: 87.4 us -> 9.62 us
  Pallas kernels: 0 us -> 42.3 us
  between operations: 15.7 us -> 0.79 us
    unnamed x4 -> x0, waiting for transfers between devices: 146 us -> none
    another operation x13 -> x3, other arithmetic: 134 us -> 0.07 us  [the longest x1 0.06 us: evidence(): gammaln(prior * 0.5 - half_steps)]
    unnamed x3 -> x0, blocking collectives: 103 us -> none
    dot_general x45 -> x0, matrix products: 82.8 us -> none  [the longest x8 59 us: one_group(): image = jnp.einsum('iksad,ktfd->iksatf', values, whiten, precision=HIGH)]
    all_gather x3 -> x1, blocking collectives: 87.2 us -> 13.1 us  [shards(): everyone = lax.all_gather(pack, 'own', axis=0, tiled=False)]
    pallas_call x0 -> x5, Pallas kernels: none -> 42.3 us  [the longest x1 15.6 us: factor(): pl.pallas_call(factor_kernel, out_shape=(jax.ShapeDtypeStruct((2, D, dept...]
    scatter x2 -> x0, local copies, waits for them, and re-layouts: 41.4 us -> none  [the longest x1 28.6 us: dispatch(): filled = jnp.zeros((n_expert * capacity,), jnp.bfloat16).at[target].set(j...]
    all_to_all x3 -> x2, waiting for transfers between devices: 29.9 us -> 66.6 us  [the longest x1 54.1 us: shards(): lax.all_to_all(outgoing.reshape(devices, chunk, D), axes, split_axis=0, c...]
  transfers between devices with their start and end apart: 6 -> 2, of which waited for: 3 -> 2; matrix products, arithmetic and copies ran while one was open for 27% -> 0% of each run, Pallas kernels for 0% -> 0%
where the time goes in v1:
time: 157 us
  waiting for transfers between devices  66.6 us (42%)
  Pallas kernels  42.3 us (27%)
  starting transfers between devices  21.9 us (14%)
  blocking collectives  13.1 us (8%)
  local copies, waits for them, and re-layouts  9.62 us (6%)
  other arithmetic  2.55 us (2%)
    all_to_all x1, waiting for transfers between devices, shards(): lax.all_to_all(outgoing.reshape(devices, chunk, D), axes, split_axis=0, c...  54.1 us
    all_to_all x1, starting transfers between devices, shards(): lax.all_to_all(outgoing.reshape(devices, chunk, D), axes, split_axis=0, c...  15.7 us
    pallas_call x1, Pallas kernels, factor(): pl.pallas_call(factor_kernel, out_shape=(jax.ShapeDtypeStruct((2, D, dept...  15.6 us
    all_gather x1, blocking collectives, shards(): everyone = lax.all_gather(pack, 'own', axis=0, tiled=False)  13.1 us
    pallas_call x1, Pallas kernels, merge(): pl.pallas_call(merge_kernel, out_shape=jax.ShapeDtypeStruct((8, D), jnp.f...  12.5 us
    all_to_all x1, waiting for transfers between devices, shards(): lax.all_to_all(outward, axes, split_axis=0, concat_axis=0, tiled=True)  12.5 us
    unnamed x16, local copies, waits for them, and re-layouts  6.83 us
    pallas_call x1, Pallas kernels, score(): pl.pallas_call(score_kernel, out_shape=jax.ShapeDtypeStruct((clusters, 1,...  6.36 us
  transfers between devices with their start and end apart: 2, of which 2 were waited for; matrix products, arithmetic and copies ran while one was open for 0% of the time, Pallas kernels for 0%

profile of v1, /device:TPU:1, one launch (start us, length us, event | category | flops | bytes accessed | tf_op | source)
XLA Modules:
  0.0 156.8 jit_solution(1107974146012562635)
XLA Ops:
  0.6 1.2 copy-done.3
  1.9 0.7 copy-done.4
  2.6 6.1 %shard_map.67 = (s32[32,128]{1,0:T(8,128)S(1)}, bf16[8192,128]{1,0:T(8,128)(2,1)S(1)}) custom-call(s32[32,128]{1,0:T(8,128)S(1)} %bitcast.9, bf16[4096,128]{1,0:T(8,128)(2,1)S(1)} %copy-done.3), custom_call_target="tpu_custom_call" | custom-call | tf_op jit(solution)/shard_map/pallas_call | solution.py:72
  8.7 1.3 copy-done.2
  10.1 0.6 copy-done.5
  10.7 15.7 %all-to-all-start = ((bf16[256,32,128]{2,1,0:T(8,128)(2,1)}), bf16[256,32,128]{2,1,0:T(8,128)(2,1)S(1)}, u32[]{:S(2)}, u32[]{:S(2)}) async-start(bf16[256,32,128]{2,1,0:T(8,128)(2,1)} %bitcast.8), calls=%async_computation | async-start | bytes 4194304 | tf_op jit(solution)/shard_map/all_to_all | solution.py:365
  26.4 0.1 dynamic_slice.3.logit_ref
  26.5 54.1 %all-to-all-done.rows_ref = bf16[256,32,128]{2,1,0:T(8,128)(2,1)S(1)} async-done(((bf16[256,32,128]{2,1,0:T(8,128)(2,1)}), bf16[256,32,128]{2,1,0:T(8,128)(2,1)S(1)}, u32[]{:S(2)}, u32[]{:S(2)}) %all-to-all-start) | async-done | bytes 2097184 | tf_op jit(solution)/shard_map/all_to_all | solution.py:365
  80.7 15.6 %shard_map.68 = (bf16[2,128,4096]{2,1,0:T(8,128)(2,1)S(1)}, bf16[2,3,256,128]{3,2,1,0:T(8,128)(2,1)S(1)}, f32[2,256,128]{2,1,0:T(8,128)S(1)}, f32[2,8,128]{2,1,0...) custom-call(f32[2]{0:T(128)S(1)} %dynamic_slice.3.logit_ref, bf16[256,32,128]{2,1,0:T(8,128)(2,1)S(1)} %all-to-all-done.rows_ref), custom_call_target="tpu_custom_call" | custom-call | tf_op jit(solution)/shard_map/pallas_call | solution.py:207
  96.3 1.4 copy-done
  97.6 13.1 %all-gather = f32[1088,128]{1,0:T(8,128)S(1)} all-gather(f32[136,128]{1,0:T(8,128)S(1)} %get-tuple-element.18.own_ref), channel_id=2, replica_groups=mesh['rows'=32,'own'=8] {'own'}, dimensions={0}, use_global_device_ids=true | all-gather | bytes 626688 | tf_op jit(solution)/shard_map/all_gather | solution.py:370
  110.7 12.5 %shard_map.71 = f32[8,128]{1,0:T(8,128)S(1)} custom-call(s32[2]{0:T(128)S(1)} %and_select_fusion.mate_ref, f32[136,128]{1,0:T(8,128)S(1)} %get-tuple-element.18.own_ref, f32[8,136,128]{2,1,0:T(8,128)S(1)} %bitcast.6, f32[8,136,128]{2,1,0:T(8,128)S(1)} %bitcast.7), custom_call_target="tpu_custom_call" | custom-call | tf_op jit(solution)/shard_map/pallas_call | solution.py:288
  123.2 0.2 add_reduce_fusion
  123.4 0.1 slice_reduce_fusion.1
  123.5 0.1 fusion.58
  123.6 0.2 fusion.7
  123.9 0.1 fusion.49
  124.3 0.1 lgamma.1181
  124.5 0.1 slice_reduce_fusion.2
  124.6 1.6 %copy-done.1 = bf16[2,128,4096]{2,1,0:T(8,128)(2,1)S(1)} copy-done((bf16[2,128,4096]{2,1,0:T(8,128)(2,1)S(1)}, bf16[2,128,4096]{2,1,0:T(8,128)(2,1)}, u32[]{:S(2)}) %copy-start.1) | copy-done | bytes 2097176
  126.2 6.4 %shard_map.69 = f32[2,1,4096]{2,1,0:T(1,128)S(1)} custom-call(bf16[2,128,4096]{2,1,0:T(8,128)(2,1)S(1)} %copy-done.1, bf16[2,3,256,128]{3,2,1,0:T(8,128)(2,1)S(1)} %get-tuple-element.13.maps_ref, f32[2,256,128]{2,1,0:T(8,128)S(1)} %get-tuple-element.14.shift_ref, f32[2,8,128]{2,1,0:T(8,128)S(1)} %get-tuple-element.15.const_ref), custom_call_target="tpu_custom_call" | custom-call | tf_op jit(solution)/shard_map/pallas_call | solution.py:243
  132.6 0.1 reduce
  132.7 0.1 reshape.146
  132.8 0.1 copy.12
  132.9 0.8 copy.13
  133.7 6.2 %all-to-all-start.1 = ((f32[256,1,32]{2,1,0:T(1,128)}), f32[256,1,32]{2,1,0:T(1,128)S(1)}, u32[]{:S(2)}, u32[]{:S(2)}) async-start(f32[256,1,32]{2,1,0:T(1,128)} %copy.13), calls=%async_computation.1 | async-start | bytes 262144 | tf_op jit(solution)/shard_map/all_to_all | solution.py:373
  139.9 0.6 subtract_multiply_fusion
  140.5 12.5 %all-to-all-done.1 = f32[256,1,32]{2,1,0:T(1,128)S(1)} async-done(((f32[256,1,32]{2,1,0:T(1,128)}), f32[256,1,32]{2,1,0:T(1,128)S(1)}, u32[]{:S(2)}, u32[]{:S(2)}) %all-to-all-start.1) | async-done | bytes 32800 | tf_op jit(solution)/shard_map/all_to_all | solution.py:373
  152.9 0.5 broadcast.500
  153.4 1.0 reduce.20
  154.4 0.7 reshape.147.table_ref
  155.1 1.7 %shard_map.70 = f32[32,128]{1,0:T(8,128)} custom-call(f32[64,128]{1,0:T(8,128)} %reshape.147.table_ref, s32[32,128]{1,0:T(8,128)} %copy-done.5), custom_call_target="tpu_custom_call" | custom-call | tf_op jit(solution)/shard_map/pallas_call | solution.py:321
  (20 shorter events, 0.5 us)
Async XLA Ops:
  0.6 1.2 copy-start.3
  1.9 0.7 copy-start.4
  8.7 1.4 copy-start.2
  10.1 0.6 copy-start.5
  10.7 15.7 %copy-start.6 = (f32[64]{0:T(128)S(1)}, f32[64]{0:T(128)}, u32[]{:S(2)}) copy-start(f32[64]{0:T(128)} %param.6) | copy-start | bytes 772
  10.7 15.8 %copy-start.7 = (s32[2]{0:T(128)S(1)}, s32[2]{0:T(128)}, u32[]{:S(2)}) copy-start(s32[2]{0:T(128)} %param.7) | copy-start | bytes 28
  10.7 70.0 %all-to-all-start = ((bf16[256,32,128]{2,1,0:T(8,128)(2,1)}), bf16[256,32,128]{2,1,0:T(8,128)(2,1)S(1)}, u32[]{:S(2)}, u32[]{:S(2)}) async-start(bf16[256,32,128]{2,1,0:T(8,128)(2,1)} %bitcast.8), calls=%async_computation | async-start | bytes 4194304 | tf_op jit(solution)/shard_map/all_to_all | solution.py:365
  96.3 1.4 copy-start
  124.6 1.6 %copy-start.1 = (bf16[2,128,4096]{2,1,0:T(8,128)(2,1)S(1)}, bf16[2,128,4096]{2,1,0:T(8,128)(2,1)}, u32[]{:S(2)}) copy-start(bf16[2,128,4096]{2,1,0:T(8,128)(2,1)} %copy-done) | copy-start | bytes 6291460
  133.7 19.3 %all-to-all-start.1 = ((f32[256,1,32]{2,1,0:T(1,128)}), f32[256,1,32]{2,1,0:T(1,128)S(1)}, u32[]{:S(2)}, u32[]{:S(2)}) async-start(f32[256,1,32]{2,1,0:T(1,128)} %copy.13), calls=%async_computation.1 | async-start | bytes 262144 | tf_op jit(solution)/shard_map/all_to_all | solution.py:373
